TPU v7x, 512 devices: a whole 4x8x8 slice. The times are simulated.
512 devices in a mesh: lon: 32 (over x, z_hi, core), lat: 16 (over y, z_lo).
Axes of the slice: x: 4, y: 8, z: 8 (z_hi: 4, z_lo: 2; z = z_hi * 2 + z_lo), core: 2. Of those that a mesh axis runs over, the one named last changes fastest.
Arguments:
- fields: bfloat16 [1, 64, 256, 4096], P(None, None, 'lat', 'lon'), may hold values from -6 to 6
- cotangent: bfloat16 [1, 64, 256, 4096], P(None, None, 'lat', 'lon'), may hold values from -6 to 6
- ocean_mask: int32 [256, 4096], P('lat', 'lon'), may hold values 0 or 1
- seam_partner: int32 [4096], replicated, may hold values from 0 to 4095, as said below
- depth_weight: bfloat16 [64, 7, 7], replicated, may hold values from -0.875 to 0.875
- norm_gain: bfloat16 [64], replicated, may hold values from 0.5 to 1.5
- layer_norm_bias: bfloat16 [64], replicated, may hold values from -3 to 3
- up_weight: bfloat16 [256, 64], replicated, may hold values from -0.75 to 0.75
- up_bias: bfloat16 [256], replicated, may hold values from -3 to 3
- down_weight: bfloat16 [64, 256], replicated, may hold values from -0.375 to 0.375
- layer_scale: bfloat16 [64], replicated, may hold values from 0.5 to 1.5
Outputs:
- output: bfloat16 [1, 64, 256, 4096], P(None, None, 'lat', 'lon')
- grad_fields: bfloat16 [1, 64, 256, 4096], P(None, None, 'lat', 'lon')
- grad_depth: float32 [64, 7, 7], replicated
- grad_gain: float32 [64], replicated
- grad_bias: float32 [64], replicated
- grad_up_weight: float32 [256, 64], replicated
- grad_up_bias: float32 [256], replicated
- grad_down_weight: float32 [64, 256], replicated
- grad_scale: float32 [64], replicated
Inputs may be any that keep to these rules, and one draw needn't show every extreme that they name: seam_partner[i] = (s - i) mod 4096 for one whole number s, so it is its own inverse.
All inputs are finite; a program needn't handle non-finite values. No bound on the sum of `ocean_mask` on one device may be relied on, other than what follows from the above.
Results may differ from a plain program's by a relative error of at most 0.0068.
Values may be sent and summed in bfloat16 or wider, within the bound.
A program may use at most 64 MiB of HBM per device.

v0:
```python
import math
import jax
import jax.numpy as jnp
from jax import lax
from jax.sharding import PartitionSpec as P


def extended_2(cells, sides, width, closed):
    for axis, dim in sides:
        count = lax.axis_size(axis)
        ends = count if closed else count - 1
        head = lax.slice_in_dim(cells, 0, width, axis=dim)
        tail = lax.slice_in_dim(cells, cells.shape[dim] - width, cells.shape[dim], axis=dim)
        cells = jnp.concatenate(
            [
                lax.ppermute(tail, axis, [(i, (i + 1) % count) for i in range(ends)]),
                cells,
                lax.ppermute(head, axis, [((i + 1) % count, i) for i in range(ends)]),
            ],
            axis=dim,
        )
    return cells


def gelu_slope(pre):
    cdf = 0.5 * (1.0 + lax.erf(pre / math.sqrt(2.0)))
    return cdf + pre * jnp.exp(-0.5 * pre * pre) / math.sqrt(2.0 * math.pi)


def cell_terms(
    conv, field, cot, mask, norm_gain, layer_norm_bias, up_weight, up_bias, down_weight, layer_scale
):
    mean_c = jnp.mean(conv, axis=0, keepdims=True)
    centered_input = conv - mean_c
    var_c = jnp.mean(centered_input * centered_input, axis=0, keepdims=True)
    reciprocal_deviation = lax.rsqrt(var_c + 1e-06)
    standardized_input = centered_input * reciprocal_deviation
    layer_norm_gain = norm_gain.astype(jnp.float32)[:, None]
    normalized_output = (
        standardized_input * layer_norm_gain + layer_norm_bias.astype(jnp.float32)[:, None]
    ).astype(jnp.bfloat16)
    pre = (
        jnp.dot(up_weight, normalized_output, preferred_element_type=jnp.float32)
        + up_bias.astype(jnp.float32)[:, None]
    )
    hidden = jax.nn.gelu(pre, approximate=False).astype(jnp.bfloat16)
    branch = jnp.dot(down_weight, hidden, preferred_element_type=jnp.float32)
    scale = layer_scale.astype(jnp.float32)[:, None]
    out = (mask * (field.astype(jnp.float32) + scale * branch)).astype(jnp.bfloat16)
    grad_in = mask * cot.astype(jnp.float32)
    d_branch = (grad_in * scale).astype(jnp.bfloat16)
    g_scale = jnp.sum(grad_in * branch, axis=1)
    contract_cells = (((1,), (1,)), ((), ()))
    contract_first = (((0,), (0,)), ((), ()))
    g_down = lax.dot_general(d_branch, hidden, contract_cells, preferred_element_type=jnp.float32)
    d_hidden = lax.dot_general(
        down_weight, d_branch, contract_first, preferred_element_type=jnp.float32
    )
    d_pre = (d_hidden * gelu_slope(pre)).astype(jnp.bfloat16)
    g_up_b = jnp.sum(d_pre.astype(jnp.float32), axis=1)
    g_up_w = lax.dot_general(
        d_pre, normalized_output, contract_cells, preferred_element_type=jnp.float32
    )
    normalized_gradient = lax.dot_general(
        up_weight, d_pre, contract_first, preferred_element_type=jnp.float32
    )
    gain_gradient = jnp.sum(normalized_gradient * standardized_input, axis=1)
    g_bias = jnp.sum(normalized_gradient, axis=1)
    gradient_through_norm = normalized_gradient * layer_norm_gain
    convolution_gradient = reciprocal_deviation * (
        gradient_through_norm
        - jnp.mean(gradient_through_norm, axis=0, keepdims=True)
        - standardized_input
        * jnp.mean(gradient_through_norm * standardized_input, axis=0, keepdims=True)
    )
    return (
        out,
        convolution_gradient.astype(jnp.bfloat16),
        (gain_gradient, g_bias, g_up_w, g_up_b, g_down, g_scale),
    )


def make_picker(wanted, carry, piece):
    width = piece.shape[3]
    inside = (wanted >= 0) & (wanted < width)
    picked = jnp.take(piece, jnp.clip(wanted, 0, width - 1), axis=3)
    return jnp.where(inside[None, None, None, :], picked, carry)


def shards(
    fields,
    cotangent,
    ocean_mask,
    seam_partner,
    depth_weight,
    norm_gain,
    layer_norm_bias,
    up_weight,
    up_bias,
    down_weight,
    layer_scale,
):
    samples, chans, rows, cols = fields.shape
    total_lon = seam_partner.shape[0]
    lon_start = lax.axis_index("lon") * cols
    positions = (lon_start + jnp.arange(-3, cols + 3, dtype=jnp.int32)) % total_lon
    partner_cols = jnp.take(seam_partner, positions)
    own_partner = partner_cols[3 : cols + 3]
    is_top = lax.axis_index("lat") == lax.axis_size("lat") - 1
    weight_f = depth_weight.astype(jnp.float32)
    mask_f = ocean_mask.astype(jnp.float32)
    lon_padded = extended_2(fields, (("lon", 3),), 3, True)
    banded = extended_2(lon_padded, (("lat", 2),), 3, False)
    upper = fields[:, :, rows - 3 :, :][:, :, ::-1, :]
    fold_init = jnp.zeros((samples, chans, 3, cols + 6), jnp.bfloat16)
    folded = make_picker(partner_cols, fold_init, lax.all_gather(upper, "lon", axis=3, tiled=True))
    top_rows = jnp.where(is_top, folded, banded[:, :, rows + 3 :, :])
    extended = jnp.concatenate([banded[:, :, : rows + 3, :], top_rows], axis=2)
    conv = jnp.zeros((samples, chans, rows, cols), jnp.float32)
    for row_tap in range(7):
        for col_tap in range(7):
            conv = conv + weight_f[:, row_tap, col_tap][None, :, None, None] * extended[
                :, :, row_tap : row_tap + rows, col_tap : col_tap + cols
            ].astype(jnp.float32)
    mask_flat = mask_f.reshape(1, rows * cols)
    out_s, dconv_s, parts = cell_terms(
        conv[0].reshape(chans, rows * cols),
        fields[0].reshape(chans, rows * cols),
        cotangent[0].reshape(chans, rows * cols),
        mask_flat,
        norm_gain,
        layer_norm_bias,
        up_weight,
        up_bias,
        down_weight,
        layer_scale,
    )
    outputs = [out_s.reshape(chans, rows, cols)]
    dconv_list = [dconv_s.reshape(chans, rows, cols)]
    output = jnp.stack(outputs)
    convolution_gradient = jnp.stack(dconv_list)
    d_conv_f = convolution_gradient.astype(jnp.float32)
    taps = []
    for row_tap in range(7):
        line = []
        for col_tap in range(7):
            line.append(
                jnp.sum(
                    d_conv_f
                    * extended[:, :, row_tap : row_tap + rows, col_tap : col_tap + cols].astype(
                        jnp.float32
                    ),
                    axis=(0, 2, 3),
                )
            )
        taps.append(jnp.stack(line, axis=1))
    g_depth = jnp.stack(taps, axis=1)
    lon_back = extended_2(convolution_gradient, (("lon", 3),), 3, True)
    band_back = extended_2(lon_back, (("lat", 2),), 3, False)
    deeper = jnp.pad(band_back, ((0, 0), (0, 0), (0, 3), (0, 0)))
    spread = jnp.zeros((samples, chans, rows + 3, cols), jnp.float32)
    for row_tap in range(7):
        for col_tap in range(7):
            spread = spread + weight_f[:, row_tap, col_tap][None, :, None, None] * deeper[
                :, :, 6 - row_tap : 9 - row_tap + rows, 6 - col_tap : 6 - col_tap + cols
            ].astype(jnp.float32)
    own = spread[:, :, :rows, :]
    margin = spread[:, :, rows:, :]
    back_init = jnp.zeros((samples, chans, 3, cols), jnp.float32)
    back = make_picker(
        own_partner,
        back_init,
        lax.all_gather(margin.astype(jnp.bfloat16), "lon", axis=3, tiled=True).astype(jnp.float32),
    )
    extra = back[:, :, ::-1, :]
    own = own.at[:, :, rows - 3 :, :].add(jnp.where(is_top, extra, 0.0))
    grad_fields = (mask_f[None, None] * cotangent.astype(jnp.float32) + own).astype(jnp.bfloat16)
    gain_gradient, g_bias, g_up_w, g_up_b, g_down, g_scale = parts
    summed = lax.psum(
        (g_depth, gain_gradient, g_bias, g_up_w, g_up_b, g_down, g_scale), ("lon", "lat")
    )
    return (
        output,
        grad_fields,
        summed[0],
        summed[1],
        summed[2],
        summed[3],
        summed[4],
        summed[5],
        summed[6],
    )


def solution(mesh):
    placed = (
        P(None, None, "lat", "lon"),
        P(None, None, "lat", "lon"),
        P("lat", "lon"),
        P(),
        P(),
        P(),
        P(),
        P(),
        P(),
        P(),
        P(),
    )
    return jax.shard_map(
        shards,
        mesh=mesh,
        in_specs=placed,
        out_specs=(
            P(None, None, "lat", "lon"),
            P(None, None, "lat", "lon"),
            P(),
            P(),
            P(),
            P(),
            P(),
            P(),
            P(),
        ),
        check_vma=False,
    )
```

profile of v0, /device:TPU:1, one launch (start us, length us, event | category | flops | bytes accessed | tf_op | source)
XLA Modules:
  0.0 497.8 jit_solution(14033838073368291433)
XLA Ops:
  7.3 1.0 slice.730
  8.3 0.6 rev.6
  9.0 1.5 copy.94
  10.5 7.2 %collective-permute-start = (bf16[1,64,16,3]{1,2,3,0:T(8,128)(2,1)S(1)}, bf16[1,64,16,3]{1,2,3,0:T(8,128)(2,1)S(1)}, u32[]{:S(2)}, u32[]{:S(2)}) collective-permute-start(bf16[1,64,16,3]{1,2,3,0:T(8,128)(2,1)S(1)} %get-tuple-element.147), channel_id=1, source_target_pairs={{0,16},{16,32},{32,48},{48,64},{64,80},{80,96},{96,112},{112,128},... | collective-permute-start | bytes 18440 | tf_op jit(solution)/shard_map/ppermute | solution.py:16
  17.7 3.5 collective-permute-start.1
  21.3 0.7 convert_element_type.421
  22.0 2.0 gather_fusion
  24.0 0.7 compare_and_fusion
  24.8 0.6 slice_bitcast_fusion.48
  25.5 0.7 slice_bitcast_fusion.47
  26.2 0.6 fusion.138
  27.0 1.3 collective-permute-start.3
  28.3 0.6 pad_clamp_fusion
  28.9 1.4 copy.95
  30.3 0.5 convert_element_type.471
  31.3 0.6 convert_element_type.474
  31.9 1.1 copy.108
  33.5 4.2 collective-permute-start.2
  37.7 42.1 %all-gather.3.cloned.1.call-done = bf16[1,64,3,4096]{3,1,2,0:T(8,128)(2,1)} async-done(((bf16[1,64,3,128]{3,1,2,0:T(8,128)(2,1)}), bf16[1,64,3,4096]{3,1,2,0:T(8,128)(2,1)}) %all-gather.3.cloned.1.call-update) | async-done | bytes 1572880 | tf_op jit(solution)/shard_map/all_gather | solution.py:116
  79.8 6.4 %copy.102 = bf16[1,64,3,4096]{1,2,3,0:T(4,128)(2,1)} copy(bf16[1,64,3,4096]{3,1,2,0:T(8,128)(2,1)} %all-gather.3.cloned.1.call-done) | data formatting | bytes 3145728 | tf_op jit(solution)/shard_map/all_gather | solution.py:116
  86.2 3.0 gather_fusion.1
  90.4 10.0 %fusion.134 = (f32[16,128]{0,1:T(8,128)S(1)}, f32[1,64,16,128]{1,2,3,0:T(8,128)S(1)}) fusion(bf16[1,64,19,134]{1,2,3,0:T(8,128)(2,1)S(1)} %get-tuple-element.142, f32[64]{0:T(128)S(1)} %get-tuple-element.152, f32[64]{0:T(128)S(1)} %get-tuple-element.153, f32[64]{0:T(128)S(1)} %get-tuple-element.154, f32[64]{0:T(128)S(1)} %get-tuple-element.155, ...), kind=kLoop, calls=%fused_computation.375 | loop fusion | flops 20051968 | bytes 11829504 | tf_op jit(solution)/shard_map/reduce_sum | solution.py:33
  100.4 1.3 copy.103
  101.9 0.7 multiply_reduce_fusion
  102.8 6.9 %fusion.5 = (bf16[256,2048]{0,1:T(8,128)(2,1)}, f32[256,2048]{0,1:T(8,128)S(1)}) fusion(f32[256]{0:T(256)S(1)} %copy-done.99, bf16[256,64]{0,1:T(8,128)(2,1)S(1)} %copy-done, f32[64]{0:T(128)S(1)} %copy-done.94, f32[64]{0:T(128)S(1)} %copy-done.85, f32[2048]{0:T(1024)S(1)} %rsqrt_bitcast_fusion, f32[2048]{0:T(1024)S(1)} %get-tuple-element.202, ...), kind=kOutput, calls=%fused_computation.63 | convolution fusion | flops 102367232 | bytes 3720704 | tf_op jit(solution)/shard_map/dot_general | solution.py:43
  109.7 2.0 convert_reduce_fusion
  111.7 1.1 fusion.121
  113.6 0.7 copy-done.12
  114.3 0.5 copy.114
  114.9 1.0 copy.109
  115.9 4.1 fusion.113
  120.2 3.2 collective-permute-start.4
  123.4 2.1 collective-permute-start.5
  125.5 1.6 fusion.112
  127.1 7.3 %collective-permute-done.5 = bf16[1,64,16,3]{3,1,2,0:T(8,128)(2,1)S(1)} collective-permute-done((bf16[1,64,16,3]{3,1,2,0:T(8,128)(2,1)S(1)}, bf16[1,64,16,3]{3,1,2,0:T(8,128)(2,1)S(1)}, u32[]{:S(2)}, u32[]{:S(2)}) %collective-permute-start.5) | collective-permute-done | bytes 6176 | tf_op jit(solution)/shard_map/ppermute | solution.py:18
  134.4 0.8 pad_maximum_fusion.8
  135.2 1.9 collective-permute-start.6
  137.2 1.3 collective-permute-start.7
  138.5 1.2 multiply_reduce_fusion.1
  139.7 0.7 reduce_sum.567
  140.3 0.7 copy.119
  141.3 1.3 stack.253
  142.6 1.3 stack.244
  143.9 1.3 stack.235
  145.2 1.4 pad_maximum_fusion.1
  146.7 1.8 pad_maximum_fusion.2
  148.7 6.7 %multiply_add_fusion = f32[1,64,19,128]{3,1,2,0:T(8,128)S(1)} fusion(bf16[1,64,19,134]{3,1,2,0:T(8,128)(2,1)S(1)} %get-tuple-element.138, bf16[1,64,22,134]{3,1,2,0:T(8,128)(2,1)S(1)} %pad_maximum_fusion.1, bf16[1,64,19,134]{3,1,2,0:T(8,128)(2,1)S(1)} %get-tuple-element.137, f32[64]{0:T(128)S(1)} %copy-done.53, f32[64]{0:T(128)S(1)} %copy-done.55, ...), kind=kLoop, calls=%fused_computation.239 | loop fusion | flops 22724608 | bytes 10078720 | tf_op jit(solution)/shard_map/add | solution.py:164
  155.4 0.9 copy-done.10
  156.3 0.6 slice.1226
  157.0 1.2 fusion.92
  158.3 3.9 fusion.85
  162.2 0.7 stack.217
  163.0 0.7 stack.208
  163.7 0.7 stack.199
  164.5 1.7 fusion.132
  166.1 2.3 fusion.133
  168.5 107.1 %all-reduce.1 = (f32[64,7,7]{0,2,1:T(8,128)}, f32[64]{0:T(128)}, f32[64]{0:T(128)}, f32[256]{0:T(256)}, f32[64]{0:T(128)}) all-reduce(f32[64,7,7]{0,2,1:T(8,128)S(1)} %constant_dynamic-update-slice_fusion, f32[64]{0:T(128)S(1)} %copy-done.92, f32[64]{0:T(128)S(1)} %copy-done.91, ...), channel_id=1, replica_groups=mesh['lon'=32,'lat'=16] {'lon','lat'}, use_global_device_ids=true, to_apply=%region_53.54 | all-reduce | flops 3584 | bytes 28672 | tf_op jit(solution)/shard_map/psum | solution.py:179
  275.6 6.4 %copy.112 = bf16[1,64,3,4096]{1,2,3,0:T(4,128)(2,1)} copy(bf16[1,64,3,4096]{3,1,2,0:T(8,128)(2,1)} %all-gather.5.cloned.1.call-done) | data formatting | bytes 3145728 | tf_op jit(solution)/shard_map/all_gather | solution.py:173
  282.1 6.3 %bitcast_convert_fusion = f32[64,3,4096]{0,1,2:T(4,128)} fusion(bf16[1,64,3,4096]{1,2,3,0:T(4,128)(2,1)} %copy.112), kind=kLoop, calls=%fused_computation.52 | loop fusion | flops 786432 | bytes 4718592 | tf_op jit(solution)/shard_map/convert_element_type | solution.py:173
  288.3 4.3 gather_fusion.2
  292.9 0.9 copy.115
  293.8 194.5 %all-reduce.5.cloned.1.call-done = (f32[256,64]{0,1:T(8,128)}, f32[64,256]{1,0:T(8,128)}) async-done(((f32[256,64]{0,1:T(8,128)}, f32[64,256]{1,0:T(8,128)}), (f32[256,64]{0,1:T(8,128)}, f32[64,256]{1,0:T(8,128)})) %all-reduce.5.cloned.1.call-update) | async-done | bytes 131088 | tf_op jit(solution)/shard_map/psum | solution.py:179
  488.3 1.5 copy.159
  489.8 1.5 copy.160
  (250 shorter events, 4.2 us)
Async XLA Ops:
  7.2 95.5 %copy-start = (bf16[256,64]{0,1:T(8,128)(2,1)S(1)}, bf16[256,64]{0,1:T(8,128)(2,1)}, u32[]{:S(2)}) copy-start(bf16[256,64]{0,1:T(8,128)(2,1)} %param.20) | copy-start | bytes 98308
  7.2 19.0 %copy-start.27 = (s32[16,128]{1,0:T(8,128)S(1)}, s32[16,128]{1,0:T(8,128)}, u32[]{:S(2)}) copy-start(s32[16,128]{1,0:T(8,128)} %param.15) | copy-start | bytes 24580
  7.2 19.6 %copy-start.16 = (bf16[1,64,16,128]{3,2,1,0:T(8,128)(2,1)S(1)}, bf16[1,64,16,128]{3,2,1,0:T(8,128)(2,1)}, u32[]{:S(2)}) copy-start(bf16[1,64,16,128]{3,2,1,0:T(8,128)(2,1)} %param.14) | copy-start | bytes 786436
  7.2 72.6 %all-gather.3.cloned.1.call-start = ((), (), s32[]{:S(2)}) async-start(), calls=%async_computation | async-start | bytes 1622016 | tf_op jit(solution)/shard_map/all_gather | solution.py:116
  8.9 266.7 %all-gather.5.cloned.1.call-start = ((), (), s32[]{:S(2)}) async-start(), calls=%async_computation.1 | async-start | bytes 1622016 | tf_op jit(solution)/shard_map/all_gather | solution.py:173
  10.5 19.8 %copy-start.95 = (bf16[64]{0:T(256)(128)(2,1)S(1)}, bf16[64]{0:T(256)(128)(2,1)}, u32[]{:S(2)}) copy-start(bf16[64]{0:T(256)(128)(2,1)} %param.18) | copy-start | bytes 388
  10.5 20.3 %copy-start.96 = (bf16[64]{0:T(256)(128)(2,1)S(1)}, bf16[64]{0:T(256)(128)(2,1)}, u32[]{:S(2)}) copy-start(bf16[64]{0:T(256)(128)(2,1)} %param.19) | copy-start | bytes 388
  10.5 20.8 %copy-start.97 = (bf16[256]{0:T(256)(128)(2,1)S(1)}, bf16[256]{0:T(256)(128)(2,1)}, u32[]{:S(2)}) copy-start(bf16[256]{0:T(256)(128)(2,1)} %param.21) | copy-start | bytes 1540
  10.5 16.3 %collective-permute-start = (bf16[1,64,16,3]{1,2,3,0:T(8,128)(2,1)S(1)}, bf16[1,64,16,3]{1,2,3,0:T(8,128)(2,1)S(1)}, u32[]{:S(2)}, u32[]{:S(2)}) collective-permute-start(bf16[1,64,16,3]{1,2,3,0:T(8,128)(2,1)S(1)} %get-tuple-element.147), channel_id=1, source_target_pairs={{0,16},{16,32},{32,48},{48,64},{64,80},{80,96},{96,112},{112,128},... | collective-permute-start | bytes 18440 | tf_op jit(solution)/shard_map/ppermute | solution.py:16
  17.7 9.1 %collective-permute-start.1 = (bf16[1,64,16,3]{1,2,3,0:T(8,128)(2,1)S(1)}, bf16[1,64,16,3]{1,2,3,0:T(8,128)(2,1)S(1)}, u32[]{:S(2)}, u32[]{:S(2)}) collective-permute-start(bf16[1,64,16,3]{1,2,3,0:T(8,128)(2,1)S(1)} %get-tuple-element.148), channel_id=1, source_target_pairs={{16,0},{32,16},{48,32},{64,48},{80,64},{96,80},{112,96},{128,112},... | collective-permute-start | bytes 18440 | tf_op jit(solution)/shard_map/ppermute | solution.py:18
  24.0 9.1 %copy-start.98 = (bf16[64]{0:T(256)(128)(2,1)S(1)}, bf16[64]{0:T(256)(128)(2,1)}, u32[]{:S(2)}) copy-start(bf16[64]{0:T(256)(128)(2,1)} %param.23) | copy-start | bytes 388
  24.7 65.4 %copy-start.28 = (f32[64]{0:T(128)}, f32[64]{0:T(128)S(1)}, u32[]{:S(2)}) copy-start(f32[64]{0:T(128)S(1)} %get-tuple-element.189) | copy-start | bytes 772
  24.7 65.4 %copy-start.30 = (f32[64]{0:T(128)}, f32[64]{0:T(128)S(1)}, u32[]{:S(2)}) copy-start(f32[64]{0:T(128)S(1)} %get-tuple-element.190) | copy-start | bytes 772
  24.7 65.4 %copy-start.32 = (f32[64]{0:T(128)}, f32[64]{0:T(128)S(1)}, u32[]{:S(2)}) copy-start(f32[64]{0:T(128)S(1)} %get-tuple-element.191) | copy-start | bytes 772
  24.7 65.4 %copy-start.34 = (f32[64]{0:T(128)}, f32[64]{0:T(128)S(1)}, u32[]{:S(2)}) copy-start(f32[64]{0:T(128)S(1)} %get-tuple-element.192) | copy-start | bytes 772
  24.7 65.4 %copy-start.36 = (f32[64]{0:T(128)}, f32[64]{0:T(128)S(1)}, u32[]{:S(2)}) copy-start(f32[64]{0:T(128)S(1)} %get-tuple-element.193) | copy-start | bytes 772
  24.7 65.4 %copy-start.38 = (f32[64]{0:T(128)}, f32[64]{0:T(128)S(1)}, u32[]{:S(2)}) copy-start(f32[64]{0:T(128)S(1)} %get-tuple-element.194) | copy-start | bytes 772
  24.7 65.4 %copy-start.40 = (f32[64]{0:T(128)}, f32[64]{0:T(128)S(1)}, u32[]{:S(2)}) copy-start(f32[64]{0:T(128)S(1)} %get-tuple-element.195) | copy-start | bytes 772
  24.8 65.4 %copy-start.42 = (f32[64]{0:T(128)}, f32[64]{0:T(128)S(1)}, u32[]{:S(2)}) copy-start(f32[64]{0:T(128)S(1)} %get-tuple-element.196) | copy-start | bytes 772
  24.8 65.4 %copy-start.44 = (f32[64]{0:T(128)}, f32[64]{0:T(128)S(1)}, u32[]{:S(2)}) copy-start(f32[64]{0:T(128)S(1)} %get-tuple-element.197) | copy-start | bytes 772
  24.8 65.4 %copy-start.46 = (f32[64]{0:T(128)}, f32[64]{0:T(128)S(1)}, u32[]{:S(2)}) copy-start(f32[64]{0:T(128)S(1)} %get-tuple-element.198) | copy-start | bytes 772
  24.8 65.4 %copy-start.48 = (f32[64]{0:T(128)}, f32[64]{0:T(128)S(1)}, u32[]{:S(2)}) copy-start(f32[64]{0:T(128)S(1)} %get-tuple-element.199) | copy-start | bytes 772
  25.4 64.8 %copy-start.50 = (f32[64]{0:T(128)}, f32[64]{0:T(128)S(1)}, u32[]{:S(2)}) copy-start(f32[64]{0:T(128)S(1)} %get-tuple-element.151) | copy-start | bytes 772
  25.4 64.8 %copy-start.52 = (f32[64]{0:T(128)}, f32[64]{0:T(128)S(1)}, u32[]{:S(2)}) copy-start(f32[64]{0:T(128)S(1)} %get-tuple-element.152) | copy-start | bytes 772
  25.4 64.8 %copy-start.54 = (f32[64]{0:T(128)}, f32[64]{0:T(128)S(1)}, u32[]{:S(2)}) copy-start(f32[64]{0:T(128)S(1)} %get-tuple-element.153) | copy-start | bytes 772
  25.4 64.8 %copy-start.56 = (f32[64]{0:T(128)}, f32[64]{0:T(128)S(1)}, u32[]{:S(2)}) copy-start(f32[64]{0:T(128)S(1)} %get-tuple-element.154) | copy-start | bytes 772
  25.4 64.8 %copy-start.58 = (f32[64]{0:T(128)}, f32[64]{0:T(128)S(1)}, u32[]{:S(2)}) copy-start(f32[64]{0:T(128)S(1)} %get-tuple-element.155) | copy-start | bytes 772
  25.4 64.8 %copy-start.60 = (f32[64]{0:T(128)}, f32[64]{0:T(128)S(1)}, u32[]{:S(2)}) copy-start(f32[64]{0:T(128)S(1)} %get-tuple-element.156) | copy-start | bytes 772
  25.4 64.8 %copy-start.62 = (f32[64]{0:T(128)}, f32[64]{0:T(128)S(1)}, u32[]{:S(2)}) copy-start(f32[64]{0:T(128)S(1)} %get-tuple-element.157) | copy-start | bytes 772
  25.5 64.8 %copy-start.64 = (f32[64]{0:T(128)}, f32[64]{0:T(128)S(1)}, u32[]{:S(2)}) copy-start(f32[64]{0:T(128)S(1)} %get-tuple-element.158) | copy-start | bytes 772
  25.5 64.8 %copy-start.66 = (f32[64]{0:T(128)}, f32[64]{0:T(128)S(1)}, u32[]{:S(2)}) copy-start(f32[64]{0:T(128)S(1)} %get-tuple-element.159) | copy-start | bytes 772
  25.5 64.8 %copy-start.68 = (f32[64]{0:T(128)}, f32[64]{0:T(128)S(1)}, u32[]{:S(2)}) copy-start(f32[64]{0:T(128)S(1)} %get-tuple-element.160) | copy-start | bytes 772
  25.5 64.8 %copy-start.70 = (f32[64]{0:T(128)}, f32[64]{0:T(128)S(1)}, u32[]{:S(2)}) copy-start(f32[64]{0:T(128)S(1)} %get-tuple-element.161) | copy-start | bytes 772
  25.5 64.8 %copy-start.72 = (f32[64]{0:T(128)}, f32[64]{0:T(128)S(1)}, u32[]{:S(2)}) copy-start(f32[64]{0:T(128)S(1)} %get-tuple-element.162) | copy-start | bytes 772
  25.5 64.8 %copy-start.74 = (f32[64]{0:T(128)}, f32[64]{0:T(128)S(1)}, u32[]{:S(2)}) copy-start(f32[64]{0:T(128)S(1)} %get-tuple-element.163) | copy-start | bytes 772
  26.8 82.9 %copy-start.18 = (f32[2048]{0:T(1024)}, f32[2048]{0:T(1024)S(1)}, u32[]{:S(2)}) copy-start(f32[2048]{0:T(1024)S(1)} %get-tuple-element.201) | copy-start | bytes 24580
  27.0 62.2 %collective-permute-start.3 = (bf16[1,64,3,134]{1,2,3,0:T(4,128)(2,1)S(1)}, bf16[1,64,3,134]{1,2,3,0:T(4,128)(2,1)S(1)}, u32[]{:S(2)}, u32[]{:S(2)}) collective-permute-start(bf16[1,64,3,134]{1,2,3,0:T(4,128)(2,1)S(1)} %get-tuple-element.144), channel_id=1, source_target_pairs={{1,0},{2,1},{3,2},{4,3},{5,4},{6,5},{7,6},{8,7},{9,8},{10,9},{11,1... | collective-permute-start | bytes 154376 | tf_op jit(solution)/shard_map/ppermute | solution.py:18
  33.5 56.1 %collective-permute-start.2 = (bf16[1,64,3,134]{1,2,3,0:T(4,128)(2,1)S(1)}, bf16[1,64,3,134]{1,2,3,0:T(4,128)(2,1)S(1)}, u32[]{:S(2)}, u32[]{:S(2)}) collective-permute-start(bf16[1,64,3,134]{1,2,3,0:T(4,128)(2,1)S(1)} %get-tuple-element.143), channel_id=1, source_target_pairs={{0,1},{1,2},{2,3},{3,4},{4,5},{5,6},{6,7},{7,8},{8,9},{9,10},{10,1... | collective-permute-start | bytes 154376 | tf_op jit(solution)/shard_map/ppermute | solution.py:16
  120.2 6.9 %collective-permute-start.4 = (bf16[1,64,16,3]{3,1,2,0:T(8,128)(2,1)S(1)}, bf16[1,64,16,3]{3,1,2,0:T(8,128)(2,1)S(1)}, u32[]{:S(2)}, u32[]{:S(2)}) collective-permute-start(bf16[1,64,16,3]{3,1,2,0:T(8,128)(2,1)S(1)} %get-tuple-element.149), channel_id=1, source_target_pairs={{0,16},{16,32},{32,48},{48,64},{64,80},{80,96},{96,112},{112,128},... | collective-permute-start | bytes 18440 | tf_op jit(solution)/shard_map/ppermute | solution.py:16
  123.3 15.1 %copy-start.5 = (f32[1,64,16,128]{3,2,1,0:T(8,128)S(1)}, f32[1,64,16,128]{3,2,1,0:T(8,128)}, u32[]{:S(2)}) copy-start(f32[1,64,16,128]{3,2,1,0:T(8,128)} %copy.108) | copy-start | bytes 1572868
  123.3 15.1 %copy-start.7 = (bf16[256,2048]{0,1:T(8,128)(2,1)S(1)}, bf16[256,2048]{0,1:T(8,128)(2,1)}, u32[]{:S(2)}) copy-start(bf16[256,2048]{0,1:T(8,128)(2,1)} %get-tuple-element.205) | copy-start | bytes 3145732
  123.4 15.1 %copy-start.15 = (f32[1,64,16,128]{3,2,1,0:T(8,128)S(1)}, f32[1,64,16,128]{3,2,1,0:T(8,128)}, u32[]{:S(2)}) copy-start(f32[1,64,16,128]{3,2,1,0:T(8,128)} %copy.95) | copy-start | bytes 1572868
  123.4 15.1 %copy-start.19 = (f32[2048]{0:T(1024)S(1)}, f32[2048]{0:T(1024)}, u32[]{:S(2)}) copy-start(f32[2048]{0:T(1024)} %copy-done.18) | copy-start | bytes 24580
  123.4 15.1 %copy-start.22 = (bf16[64,256]{1,0:T(8,128)(2,1)S(1)}, bf16[64,256]{1,0:T(8,128)(2,1)}, u32[]{:S(2)}) copy-start(bf16[64,256]{1,0:T(8,128)(2,1)} %param.22) | copy-start | bytes 98308
  123.4 15.1 %copy-start.87 = (f32[64]{0:T(128)S(1)}, f32[64]{0:T(128)}, u32[]{:S(2)}) copy-start(f32[64]{0:T(128)} %convert_element_type.420) | copy-start | bytes 772
  123.4 11.0 %collective-permute-start.5 = (bf16[1,64,16,3]{3,1,2,0:T(8,128)(2,1)S(1)}, bf16[1,64,16,3]{3,1,2,0:T(8,128)(2,1)S(1)}, u32[]{:S(2)}, u32[]{:S(2)}) collective-permute-start(bf16[1,64,16,3]{3,1,2,0:T(8,128)(2,1)S(1)} %get-tuple-element.150), channel_id=1, source_target_pairs={{16,0},{32,16},{48,32},{64,48},{80,64},{96,80},{112,96},{128,112},... | collective-permute-start | bytes 18440 | tf_op jit(solution)/shard_map/ppermute | solution.py:18
  127.1 12.6 %copy-start.3 = (f32[2048,64]{0,1:T(8,128)S(1)}, f32[2048,64]{0,1:T(8,128)}, u32[]{:S(2)}) copy-start(f32[2048,64]{0,1:T(8,128)} %copy-done.2) | copy-start | bytes 1572868
  135.2 10.0 %collective-permute-start.6 = (bf16[1,64,3,134]{3,1,2,0:T(8,128)(2,1)}, bf16[1,64,3,134]{3,1,2,0:T(8,128)(2,1)}, u32[]{:S(2)}, u32[]{:S(2)}) collective-permute-start(bf16[1,64,3,134]{3,1,2,0:T(8,128)(2,1)} %get-tuple-element.140), channel_id=1, source_target_pairs={{0,1},{1,2},{2,3},{3,4},{4,5},{5,6},{6,7},{7,8},{8,9},{9,10},{10,1... | collective-permute-start | bytes 154376 | tf_op jit(solution)/shard_map/ppermute | solution.py:16
  137.2 8.1 %collective-permute-start.7 = (bf16[1,64,3,134]{3,1,2,0:T(8,128)(2,1)}, bf16[1,64,3,134]{3,1,2,0:T(8,128)(2,1)}, u32[]{:S(2)}, u32[]{:S(2)}) collective-permute-start(bf16[1,64,3,134]{3,1,2,0:T(8,128)(2,1)} %get-tuple-element.139), channel_id=1, source_target_pairs={{1,0},{2,1},{3,2},{4,3},{5,4},{6,5},{7,6},{8,7},{9,8},{10,9},{11,1... | collective-permute-start | bytes 154376 | tf_op jit(solution)/shard_map/ppermute | solution.py:18
  141.1 7.4 %copy-start.37 = (f32[64]{0:T(128)S(1)}, f32[64]{0:T(128)}, u32[]{:S(2)}) copy-start(f32[64]{0:T(128)} %copy-done.36) | copy-start | bytes 772
  141.1 7.4 %copy-start.39 = (f32[64]{0:T(128)S(1)}, f32[64]{0:T(128)}, u32[]{:S(2)}) copy-start(f32[64]{0:T(128)} %copy-done.38) | copy-start | bytes 772
  141.1 7.4 %copy-start.41 = (f32[64]{0:T(128)S(1)}, f32[64]{0:T(128)}, u32[]{:S(2)}) copy-start(f32[64]{0:T(128)} %copy-done.40) | copy-start | bytes 772
  141.1 7.4 %copy-start.43 = (f32[64]{0:T(128)S(1)}, f32[64]{0:T(128)}, u32[]{:S(2)}) copy-start(f32[64]{0:T(128)} %copy-done.42) | copy-start | bytes 772
  141.1 7.4 %copy-start.45 = (f32[64]{0:T(128)S(1)}, f32[64]{0:T(128)}, u32[]{:S(2)}) copy-start(f32[64]{0:T(128)} %copy-done.44) | copy-start | bytes 772
  141.1 7.4 %copy-start.47 = (f32[64]{0:T(128)S(1)}, f32[64]{0:T(128)}, u32[]{:S(2)}) copy-start(f32[64]{0:T(128)} %copy-done.46) | copy-start | bytes 772
  141.2 7.4 %copy-start.49 = (f32[64]{0:T(128)S(1)}, f32[64]{0:T(128)}, u32[]{:S(2)}) copy-start(f32[64]{0:T(128)} %copy-done.48) | copy-start | bytes 772
  141.2 7.4 %copy-start.51 = (f32[64]{0:T(128)S(1)}, f32[64]{0:T(128)}, u32[]{:S(2)}) copy-start(f32[64]{0:T(128)} %copy-done.50) | copy-start | bytes 772
  156.9 331.4 %all-reduce.5.cloned.1.call-start = ((), (), s32[]{:S(2)}) async-start(), calls=%async_computation.2 | async-start | bytes 262144 | tf_op jit(solution)/shard_map/psum | solution.py:179
  282.0 10.7 %copy-start.89 = (pred[128]{0:T(512)(128)(4,1)S(1)}, pred[128]{0:T(512)(128)(4,1)}, u32[]{:S(2)}) copy-start(pred[128]{0:T(512)(128)(4,1)} %get-tuple-element.131) | copy-start | bytes 388
  282.0 10.7 %copy-start.90 = (pred[128]{0:T(512)(128)(4,1)S(1)}, pred[128]{0:T(512)(128)(4,1)}, u32[]{:S(2)}) copy-start(pred[128]{0:T(512)(128)(4,1)} %get-tuple-element.204) | copy-start | bytes 388
  282.0 10.7 %copy-start.11 = (f32[1,64,19,128]{3,1,2,0:T(8,128)S(1)}, f32[1,64,19,128]{3,1,2,0:T(8,128)}, u32[]{:S(2)}) copy-start(f32[1,64,19,128]{3,1,2,0:T(8,128)} %copy-done.10) | copy-start | bytes 1867780
  282.0 10.7 %slice-start = ((f32[1,64,19,128]{3,1,2,0:T(8,128)}), f32[1,64,16,128]{3,1,2,0:T(8,128)S(1)}, s32[]{:S(2)}) async-start(f32[1,64,19,128]{3,1,2,0:T(8,128)} %copy-done.10), calls=%async_computation.3 | async-start | bytes 1048576 | tf_op jit(solution)/shard_map/slice | solution.py:167
  282.1 10.8 %copy-start.17 = (bf16[1,64,16,128]{3,2,1,0:T(8,128)(2,1)S(1)}, bf16[1,64,16,128]{3,2,1,0:T(8,128)(2,1)}, u32[]{:S(2)}) copy-start(bf16[1,64,16,128]{3,2,1,0:T(8,128)(2,1)} %param.14) | copy-start | bytes 786436
  282.1 10.8 %copy-start.23 = (f32[16,128]{1,0:T(8,128)S(1)}, f32[16,128]{1,0:T(8,128)}, u32[]{:S(2)}) copy-start(f32[16,128]{1,0:T(8,128)} %get-tuple-element.200) | copy-start | bytes 24580
  (48 other events, 263.2 us)
Sparse Core Ops, SparseCore 0:
  11.7 68.0 all-gather.2
  157.0 65.3 all-gather.4
  228.2 260.0 all-reduce.4
where the time goes:
time: 499 us; the launch traced here: 498 us
  waiting for transfers between devices  244 us (49%)
  blocking collectives  107 us (21%)
  local copies, waits for them, and re-layouts  46.1 us (9%)
  other arithmetic  45.4 us (9%)
  starting transfers between devices  24.7 us (5%)
  between operations  15.4 us (3%)
  matrix products  15.1 us (3%)
    psum x1, waiting for transfers between devices, shards(): lax.psum((g_depth, gain_gradient, g_bias, g_up_w, g_up_b, g_down, g_scale...  195 us
    psum x1, blocking collectives, shards(): lax.psum((g_depth, gain_gradient, g_bias, g_up_w, g_up_b, g_down, g_scale...  107 us
    all_gather x1, waiting for transfers between devices, shards(): lax.all_gather(upper, 'lon', axis=3, tiled=True)  42.1 us
    ppermute x4, starting transfers between devices, extended_2(): lax.ppermute(tail, axis, [(i, (i + 1) % count) for i in range(ends)])  16.4 us
    reduce_sum x4, other arithmetic, shards(): jnp.sum(d_conv_f * extended[:, :, row_tap:row_tap + rows, col_tap:col_tap...  10.9 us
    reduce_sum x1, other arithmetic, cell_terms(): mean_c = jnp.mean(conv, axis=0, keepdims=True)  9.98 us
  transfers between devices with their start and end apart: 11, of which 3 were waited for; matrix products, arithmetic and copies ran while one was open for 12% of the time, Pallas kernels for 0%

commit v1 on v0

--- a/solution.py
+++ b/solution.py
@@ -177,7 +177,7 @@
     grad_fields = (mask_f[None, None] * cotangent.astype(jnp.float32) + own).astype(jnp.bfloat16)
     gain_gradient, g_bias, g_up_w, g_up_b, g_down, g_scale = parts
     summed = lax.psum(
-        (g_depth, gain_gradient, g_bias, g_up_w, g_up_b, g_down, g_scale), ("lon", "lat")
+        lax.psum((g_depth, gain_gradient, g_bias, g_up_w, g_up_b, g_down, g_scale), "lon"), "lat"
     )
     return (
         output,

time: 499 us -> 622 us (1.25); the launches traced: 498 us -> 612 us
  blocking collectives: 107 us -> 189 us
  waiting for transfers between devices: 244 us -> 283 us
  local copies, waits for them, and re-layouts: 46.1 us -> 39.1 us
    psum x1, waiting for transfers between devices: 195 us -> 56.4 us  [shards(): lax.psum((g_depth, gain_gradient, g_bias, g_up_w, g_up_b, g_down, g_scale...]
    psum x0 -> x1, waiting for transfers between devices: none -> 111 us  [shards(): lax.psum(lax.psum((g_depth, gain_gradient, g_bias, g_up_w, g_up_b, g_down...]
    all_gather x1, waiting for transfers between devices: 0.01 us -> 61.5 us  [shards(): lax.all_gather(margin.astype(jnp.bfloat16), 'lon', axis=3, tiled=True)]
    psum x0 -> x1, blocking collectives: none -> 48.9 us  [shards(): lax.psum(lax.psum((g_depth, gain_gradient, g_bias, g_up_w, g_up_b, g_down...]
    psum x1, blocking collectives: 107 us -> 140 us  [shards(): lax.psum((g_depth, gain_gradient, g_bias, g_up_w, g_up_b, g_down, g_scale...]
  transfers between devices with their start and end apart: 11 -> 12, of which waited for: 3 -> 7; matrix products, arithmetic and copies ran while one was open for 12% -> 10% of each run, Pallas kernels for 0% -> 0%
where the time goes in v1:
time: 622 us; the launch traced here: 612 us
  waiting for transfers between devices  283 us (45%)
  blocking collectives  189 us (30%)
  other arithmetic  44.5 us (7%)
  local copies, waits for them, and re-layouts  39.1 us (6%)
  starting transfers between devices  24.9 us (4%)
  matrix products  15.7 us (3%)
  between operations  15.4 us (2%)
    psum x1, blocking collectives, shards(): lax.psum((g_depth, gain_gradient, g_bias, g_up_w, g_up_b, g_down, g_scale...  140 us
    psum x1, waiting for transfers between devices, shards(): lax.psum(lax.psum((g_depth, gain_gradient, g_bias, g_up_w, g_up_b, g_down...  111 us
    all_gather x1, waiting for transfers between devices, shards(): lax.all_gather(margin.astype(jnp.bfloat16), 'lon', axis=3, tiled=True)  61.5 us
    psum x1, waiting for transfers between devices, shards(): lax.psum((g_depth, gain_gradient, g_bias, g_up_w, g_up_b, g_down, g_scale...  56.4 us
    psum x1, blocking collectives, shards(): lax.psum(lax.psum((g_depth, gain_gradient, g_bias, g_up_w, g_up_b, g_down...  48.9 us
    all_gather x1, waiting for transfers between devices, shards(): lax.all_gather(upper, 'lon', axis=3, tiled=True)  42.4 us
    ppermute x4, starting transfers between devices, extended_2(): lax.ppermute(tail, axis, [(i, (i + 1) % count) for i in range(ends)])  16.7 us
  transfers between devices with their start and end apart: 12, of which 7 were waited for; matrix products, arithmetic and copies ran while one was open for 10% of the time, Pallas kernels for 0%

profile of v1, /device:TPU:1, one launch (start us, length us, event | category | flops | bytes accessed | tf_op | source)
XLA Modules:
  0.0 611.8 jit_solution(16386909613917631834)
XLA Ops:
  7.3 1.0 slice.730
  8.3 0.6 rev.6
  9.0 1.5 copy.94
  10.5 7.2 %collective-permute-start = (bf16[1,64,16,3]{1,2,3,0:T(8,128)(2,1)S(1)}, bf16[1,64,16,3]{1,2,3,0:T(8,128)(2,1)S(1)}, u32[]{:S(2)}, u32[]{:S(2)}) collective-permute-start(bf16[1,64,16,3]{1,2,3,0:T(8,128)(2,1)S(1)} %get-tuple-element.154), channel_id=1, source_target_pairs={{0,16},{16,32},{32,48},{48,64},{64,80},{80,96},{96,112},{112,128},... | collective-permute-start | bytes 18440 | tf_op jit(solution)/shard_map/ppermute | solution.py:16
  17.7 3.5 collective-permute-start.1
  21.3 0.7 convert_element_type.421
  22.0 2.0 gather_fusion
  24.0 0.7 compare_and_fusion
  25.0 0.6 slice_bitcast_fusion.47
  25.7 0.6 fusion.138
  26.6 1.3 collective-permute-start.3
  27.9 0.6 pad_clamp_fusion
  28.5 1.4 copy.95
  29.9 0.5 convert_element_type.471
  30.4 0.5 convert_element_type.472
  30.9 1.1 copy.108
  32.0 0.5 convert_element_type.420
  32.5 4.2 collective-permute-start.2
  36.7 42.4 %all-gather.3.cloned.1.call-done = bf16[1,64,3,4096]{3,1,2,0:T(8,128)(2,1)} async-done(((bf16[1,64,3,128]{3,1,2,0:T(8,128)(2,1)}), bf16[1,64,3,4096]{3,1,2,0:T(8,128)(2,1)}) %all-gather.3.cloned.1.call-update) | async-done | bytes 1572880 | tf_op jit(solution)/shard_map/all_gather | solution.py:116
  79.1 6.4 %copy.102 = bf16[1,64,3,4096]{1,2,3,0:T(4,128)(2,1)} copy(bf16[1,64,3,4096]{3,1,2,0:T(8,128)(2,1)} %all-gather.3.cloned.1.call-done) | data formatting | bytes 3145728 | tf_op jit(solution)/shard_map/all_gather | solution.py:116
  85.5 3.0 gather_fusion.1
  88.4 0.4 fusion.126
  88.8 0.5 maximum_maximum_fusion
  89.7 10.5 %fusion.134 = (f32[16,128]{0,1:T(8,128)S(1)}, f32[1,64,16,128]{1,2,3,0:T(8,128)S(1)}) fusion(bf16[1,64,19,134]{1,2,3,0:T(8,128)(2,1)S(1)} %get-tuple-element.149, f32[64]{0:T(128)S(1)} %get-tuple-element.159, f32[64]{0:T(128)S(1)} %get-tuple-element.160, f32[64]{0:T(128)S(1)} %get-tuple-element.161, f32[64]{0:T(128)S(1)} %get-tuple-element.162, ...), kind=kLoop, calls=%fused_computation.375 | loop fusion | flops 20051968 | bytes 11829504 | tf_op jit(solution)/shard_map/reduce_sum | solution.py:33
  100.2 1.4 copy.103
  101.8 0.6 multiply_reduce_fusion
  102.5 6.9 %fusion.5 = (bf16[256,2048]{0,1:T(8,128)(2,1)}, f32[256,2048]{0,1:T(8,128)S(1)}) fusion(f32[256]{0:T(256)S(1)} %convert_element_type.474, bf16[256,64]{0,1:T(8,128)(2,1)S(1)} %copy-done, f32[64]{0:T(128)} %convert_element_type.472, f32[64]{0:T(128)} %convert_element_type.471, f32[2048]{0:T(1024)S(1)} %rsqrt_bitcast_fusion, ...), kind=kOutput, calls=%fused_computation.63 | convolution fusion | flops 102367232 | bytes 3720704 | tf_op jit(solution)/shard_map/dot_general | solution.py:43
  109.5 2.0 convert_reduce_fusion
  111.5 1.8 fusion.121
  113.4 0.9 fusion.123
  114.4 0.7 copy-done.11
  115.1 0.5 copy.114
  115.6 1.0 copy.109
  116.6 4.4 fusion.113
  121.2 3.3 collective-permute-start.4
  124.5 1.9 collective-permute-start.5
  126.4 1.7 fusion.133
  128.2 7.2 %collective-permute-done.5 = bf16[1,64,16,3]{3,1,2,0:T(8,128)(2,1)S(1)} collective-permute-done((bf16[1,64,16,3]{3,1,2,0:T(8,128)(2,1)S(1)}, bf16[1,64,16,3]{3,1,2,0:T(8,128)(2,1)S(1)}, u32[]{:S(2)}, u32[]{:S(2)}) %collective-permute-start.5) | collective-permute-done | bytes 6176 | tf_op jit(solution)/shard_map/ppermute | solution.py:18
  135.3 0.8 pad_maximum_fusion.8
  136.2 2.1 collective-permute-start.6
  138.2 1.3 collective-permute-start.7
  139.6 1.0 fusion.132
  140.7 4.2 collective-permute-done.7
  144.8 1.4 pad_maximum_fusion.1
  146.3 1.4 pad_maximum_fusion.2
  147.8 7.0 %multiply_add_fusion = f32[1,64,19,128]{3,1,2,0:T(8,128)S(1)} fusion(bf16[1,64,19,134]{3,1,2,0:T(8,128)(2,1)S(1)} %get-tuple-element.145, bf16[1,64,22,134]{3,1,2,0:T(8,128)(2,1)S(1)} %pad_maximum_fusion.1, bf16[1,64,19,134]{3,1,2,0:T(8,128)(2,1)S(1)} %get-tuple-element.144, f32[64]{0:T(128)} %copy-done.38, f32[64]{0:T(128)} %copy-done.39, ...), kind=kLoop, calls=%fused_computation.239 | loop fusion | flops 22724608 | bytes 10072832 | tf_op jit(solution)/shard_map/add | solution.py:164
  154.8 0.9 copy-done.9
  155.6 0.6 slice.1226
  156.3 2.2 multiply_reduce_fusion.1
  158.9 0.7 copy.119
  159.6 1.0 fusion.112
  160.9 1.2 fusion.92
  162.2 3.3 fusion.85
  165.7 140.5 %all-reduce.1 = (f32[64,7,7]{0,2,1:T(8,128)S(1)}, f32[64]{0:T(128)S(1)}, f32[64]{0:T(128)S(1)}, f32[256]{0:T(256)S(1)}, f32[64]{0:T(128)S(1)}) all-reduce(f32[64,7,7]{0,2,1:T(8,128)S(1)} %constant_dynamic-update-slice_fusion, f32[64]{0:T(128)S(1)} %copy-done.87, f32[64]{0:T(128)S(1)} %reduce_sum.567, ...), channel_id=1, replica_groups=mesh['lon'=32,'lat'=16] {'lon'}, use_global_device_ids=true, to_apply=%region_53.54 | all-reduce | flops 3584 | bytes 28672 | tf_op jit(solution)/shard_map/psum | solution.py:180
  306.2 48.9 %all-reduce.3 = (f32[64,7,7]{0,2,1:T(8,128)}, f32[64]{0:T(128)}, f32[64]{0:T(128)}, f32[256]{0:T(256)}, f32[64]{0:T(128)}) all-reduce(f32[64,7,7]{0,2,1:T(8,128)S(1)} %get-tuple-element.124, f32[64]{0:T(128)S(1)} %get-tuple-element.125, f32[64]{0:T(128)S(1)} %get-tuple-element.126, ...), channel_id=1, replica_groups=mesh['lon'=32,'lat'=16] {'lat'}, use_global_device_ids=true, to_apply=%region_54.55 | all-reduce | flops 3584 | bytes 28672 | tf_op jit(solution)/shard_map/psum | solution.py:179
  355.1 56.4 %all-reduce.8.cloned.1.call-done = (f32[256,64]{0,1:T(8,128)}, f32[64,256]{1,0:T(8,128)}) async-done(((f32[256,64]{0,1:T(8,128)}, f32[64,256]{1,0:T(8,128)}), (f32[256,64]{0,1:T(8,128)}, f32[64,256]{1,0:T(8,128)})) %all-reduce.8.cloned.1.call-update) | async-done | bytes 131088 | tf_op jit(solution)/shard_map/psum | solution.py:180
  411.5 61.5 %all-gather.5.cloned.1.call-done = bf16[1,64,3,4096]{3,1,2,0:T(8,128)(2,1)} async-done(((bf16[1,64,3,128]{3,1,2,0:T(8,128)(2,1)}), bf16[1,64,3,4096]{3,1,2,0:T(8,128)(2,1)}) %all-gather.5.cloned.1.call-update) | async-done | bytes 1572880 | tf_op jit(solution)/shard_map/all_gather | solution.py:173
  473.0 6.4 %copy.112 = bf16[1,64,3,4096]{1,2,3,0:T(4,128)(2,1)} copy(bf16[1,64,3,4096]{3,1,2,0:T(8,128)(2,1)} %all-gather.5.cloned.1.call-done) | data formatting | bytes 3145728 | tf_op jit(solution)/shard_map/all_gather | solution.py:173
  479.4 6.2 %bitcast_convert_fusion = f32[64,3,4096]{0,1,2:T(4,128)} fusion(bf16[1,64,3,4096]{1,2,3,0:T(4,128)(2,1)} %copy.112), kind=kLoop, calls=%fused_computation.52 | loop fusion | flops 786432 | bytes 4718592 | tf_op jit(solution)/shard_map/convert_element_type | solution.py:173
  485.7 4.3 gather_fusion.2
  490.3 0.9 copy.115
  491.2 111.1 %all-reduce.10.cloned.1.call-done = (f32[256,64]{0,1:T(8,128)}, f32[64,256]{1,0:T(8,128)}) async-done(((f32[256,64]{0,1:T(8,128)}, f32[64,256]{1,0:T(8,128)}), (f32[256,64]{0,1:T(8,128)}, f32[64,256]{1,0:T(8,128)})) %all-reduce.10.cloned.1.call-update) | async-done | bytes 131088 | tf_op jit(solution)/shard_map/psum | solution.py:179
  602.3 1.5 copy.161
  603.8 1.5 copy.162
  (240 shorter events, 2.0 us)
Async XLA Ops:
  7.2 95.3 %copy-start = (bf16[256,64]{0,1:T(8,128)(2,1)S(1)}, bf16[256,64]{0,1:T(8,128)(2,1)}, u32[]{:S(2)}) copy-start(bf16[256,64]{0,1:T(8,128)(2,1)} %param.20) | copy-start | bytes 98308
  7.2 18.4 %copy-start.23 = (s32[16,128]{1,0:T(8,128)S(1)}, s32[16,128]{1,0:T(8,128)}, u32[]{:S(2)}) copy-start(s32[16,128]{1,0:T(8,128)} %param.15) | copy-start | bytes 24580
  7.2 19.1 %copy-start.16 = (bf16[1,64,16,128]{3,2,1,0:T(8,128)(2,1)S(1)}, bf16[1,64,16,128]{3,2,1,0:T(8,128)(2,1)}, u32[]{:S(2)}) copy-start(bf16[1,64,16,128]{3,2,1,0:T(8,128)(2,1)} %param.14) | copy-start | bytes 786436
  7.2 71.9 %all-gather.3.cloned.1.call-start = ((), (), s32[]{:S(2)}) async-start(), calls=%async_computation | async-start | bytes 1622016 | tf_op jit(solution)/shard_map/all_gather | solution.py:116
  8.9 402.6 %all-reduce.8.cloned.1.call-start = ((), (), s32[]{:S(2)}) async-start(), calls=%async_computation.2 | async-start | bytes 262144 | tf_op jit(solution)/shard_map/psum | solution.py:180
  10.5 19.4 %copy-start.89 = (bf16[64]{0:T(256)(128)(2,1)S(1)}, bf16[64]{0:T(256)(128)(2,1)}, u32[]{:S(2)}) copy-start(bf16[64]{0:T(256)(128)(2,1)} %param.18) | copy-start | bytes 388
  10.5 19.9 %copy-start.90 = (bf16[64]{0:T(256)(128)(2,1)S(1)}, bf16[64]{0:T(256)(128)(2,1)}, u32[]{:S(2)}) copy-start(bf16[64]{0:T(256)(128)(2,1)} %param.19) | copy-start | bytes 388
  10.5 20.4 %copy-start.91 = (bf16[256]{0:T(256)(128)(2,1)S(1)}, bf16[256]{0:T(256)(128)(2,1)}, u32[]{:S(2)}) copy-start(bf16[256]{0:T(256)(128)(2,1)} %param.21) | copy-start | bytes 1540
  10.5 15.9 %collective-permute-start = (bf16[1,64,16,3]{1,2,3,0:T(8,128)(2,1)S(1)}, bf16[1,64,16,3]{1,2,3,0:T(8,128)(2,1)S(1)}, u32[]{:S(2)}, u32[]{:S(2)}) collective-permute-start(bf16[1,64,16,3]{1,2,3,0:T(8,128)(2,1)S(1)} %get-tuple-element.154), channel_id=1, source_target_pairs={{0,16},{16,32},{32,48},{48,64},{64,80},{80,96},{96,112},{112,128},... | collective-permute-start | bytes 18440 | tf_op jit(solution)/shard_map/ppermute | solution.py:16
  17.7 8.7 %collective-permute-start.1 = (bf16[1,64,16,3]{1,2,3,0:T(8,128)(2,1)S(1)}, bf16[1,64,16,3]{1,2,3,0:T(8,128)(2,1)S(1)}, u32[]{:S(2)}, u32[]{:S(2)}) collective-permute-start(bf16[1,64,16,3]{1,2,3,0:T(8,128)(2,1)S(1)} %get-tuple-element.155), channel_id=1, source_target_pairs={{16,0},{32,16},{48,32},{64,48},{80,64},{96,80},{112,96},{128,112},... | collective-permute-start | bytes 18440 | tf_op jit(solution)/shard_map/ppermute | solution.py:18
  24.7 64.6 %copy-start.24 = (f32[64]{0:T(128)}, f32[64]{0:T(128)S(1)}, u32[]{:S(2)}) copy-start(f32[64]{0:T(128)S(1)} %get-tuple-element.196) | copy-start | bytes 772
  24.7 64.6 %copy-start.26 = (f32[64]{0:T(128)}, f32[64]{0:T(128)S(1)}, u32[]{:S(2)}) copy-start(f32[64]{0:T(128)S(1)} %get-tuple-element.197) | copy-start | bytes 772
  24.7 64.6 %copy-start.28 = (f32[64]{0:T(128)}, f32[64]{0:T(128)S(1)}, u32[]{:S(2)}) copy-start(f32[64]{0:T(128)S(1)} %get-tuple-element.198) | copy-start | bytes 772
  24.7 64.6 %copy-start.29 = (f32[64]{0:T(128)}, f32[64]{0:T(128)S(1)}, u32[]{:S(2)}) copy-start(f32[64]{0:T(128)S(1)} %get-tuple-element.199) | copy-start | bytes 772
  24.7 64.6 %copy-start.30 = (f32[64]{0:T(128)}, f32[64]{0:T(128)S(1)}, u32[]{:S(2)}) copy-start(f32[64]{0:T(128)S(1)} %get-tuple-element.200) | copy-start | bytes 772
  24.7 64.6 %copy-start.31 = (f32[64]{0:T(128)}, f32[64]{0:T(128)S(1)}, u32[]{:S(2)}) copy-start(f32[64]{0:T(128)S(1)} %get-tuple-element.201) | copy-start | bytes 772
  24.8 64.6 %copy-start.32 = (f32[64]{0:T(128)}, f32[64]{0:T(128)S(1)}, u32[]{:S(2)}) copy-start(f32[64]{0:T(128)S(1)} %get-tuple-element.202) | copy-start | bytes 772
  24.8 64.6 %copy-start.33 = (f32[64]{0:T(128)}, f32[64]{0:T(128)S(1)}, u32[]{:S(2)}) copy-start(f32[64]{0:T(128)S(1)} %get-tuple-element.203) | copy-start | bytes 772
  24.8 64.6 %copy-start.34 = (f32[64]{0:T(128)}, f32[64]{0:T(128)S(1)}, u32[]{:S(2)}) copy-start(f32[64]{0:T(128)S(1)} %get-tuple-element.204) | copy-start | bytes 772
  24.8 64.6 %copy-start.35 = (f32[64]{0:T(128)}, f32[64]{0:T(128)S(1)}, u32[]{:S(2)}) copy-start(f32[64]{0:T(128)S(1)} %get-tuple-element.205) | copy-start | bytes 772
  24.8 64.6 %copy-start.36 = (f32[64]{0:T(128)}, f32[64]{0:T(128)S(1)}, u32[]{:S(2)}) copy-start(f32[64]{0:T(128)S(1)} %get-tuple-element.206) | copy-start | bytes 772
  24.8 64.6 %copy-start.37 = (f32[64]{0:T(128)}, f32[64]{0:T(128)S(1)}, u32[]{:S(2)}) copy-start(f32[64]{0:T(128)S(1)} %get-tuple-element.158) | copy-start | bytes 772
  24.8 64.6 %copy-start.38 = (f32[64]{0:T(128)}, f32[64]{0:T(128)S(1)}, u32[]{:S(2)}) copy-start(f32[64]{0:T(128)S(1)} %get-tuple-element.159) | copy-start | bytes 772
  24.8 64.6 %copy-start.39 = (f32[64]{0:T(128)}, f32[64]{0:T(128)S(1)}, u32[]{:S(2)}) copy-start(f32[64]{0:T(128)S(1)} %get-tuple-element.160) | copy-start | bytes 772
  24.9 64.6 %copy-start.40 = (f32[64]{0:T(128)}, f32[64]{0:T(128)S(1)}, u32[]{:S(2)}) copy-start(f32[64]{0:T(128)S(1)} %get-tuple-element.161) | copy-start | bytes 772
  24.9 64.6 %copy-start.41 = (f32[64]{0:T(128)}, f32[64]{0:T(128)S(1)}, u32[]{:S(2)}) copy-start(f32[64]{0:T(128)S(1)} %get-tuple-element.162) | copy-start | bytes 772
  24.9 64.6 %copy-start.42 = (f32[64]{0:T(128)}, f32[64]{0:T(128)S(1)}, u32[]{:S(2)}) copy-start(f32[64]{0:T(128)S(1)} %get-tuple-element.163) | copy-start | bytes 772
  24.9 64.6 %copy-start.43 = (f32[64]{0:T(128)}, f32[64]{0:T(128)S(1)}, u32[]{:S(2)}) copy-start(f32[64]{0:T(128)S(1)} %get-tuple-element.164) | copy-start | bytes 772
  24.9 64.6 %copy-start.44 = (f32[64]{0:T(128)}, f32[64]{0:T(128)S(1)}, u32[]{:S(2)}) copy-start(f32[64]{0:T(128)S(1)} %get-tuple-element.165) | copy-start | bytes 772
  24.9 64.6 %copy-start.45 = (f32[64]{0:T(128)}, f32[64]{0:T(128)S(1)}, u32[]{:S(2)}) copy-start(f32[64]{0:T(128)S(1)} %get-tuple-element.166) | copy-start | bytes 772
  24.9 64.6 %copy-start.46 = (f32[64]{0:T(128)}, f32[64]{0:T(128)S(1)}, u32[]{:S(2)}) copy-start(f32[64]{0:T(128)S(1)} %get-tuple-element.167) | copy-start | bytes 772
  24.9 64.6 %copy-start.47 = (f32[64]{0:T(128)}, f32[64]{0:T(128)S(1)}, u32[]{:S(2)}) copy-start(f32[64]{0:T(128)S(1)} %get-tuple-element.168) | copy-start | bytes 772
  24.9 64.6 %copy-start.48 = (f32[64]{0:T(128)}, f32[64]{0:T(128)S(1)}, u32[]{:S(2)}) copy-start(f32[64]{0:T(128)S(1)} %get-tuple-element.169) | copy-start | bytes 772
  24.9 64.6 %copy-start.49 = (f32[64]{0:T(128)}, f32[64]{0:T(128)S(1)}, u32[]{:S(2)}) copy-start(f32[64]{0:T(128)S(1)} %get-tuple-element.170) | copy-start | bytes 772
  25.0 64.6 %copy-start.50 = (f32[64]{0:T(128)}, f32[64]{0:T(128)S(1)}, u32[]{:S(2)}) copy-start(f32[64]{0:T(128)S(1)} %get-tuple-element.171) | copy-start | bytes 772
  25.0 64.6 %copy-start.51 = (f32[64]{0:T(128)}, f32[64]{0:T(128)S(1)}, u32[]{:S(2)}) copy-start(f32[64]{0:T(128)S(1)} %get-tuple-element.172) | copy-start | bytes 772
  25.0 64.6 %copy-start.52 = (f32[64]{0:T(128)}, f32[64]{0:T(128)S(1)}, u32[]{:S(2)}) copy-start(f32[64]{0:T(128)S(1)} %get-tuple-element.173) | copy-start | bytes 772
  25.0 64.6 %copy-start.53 = (f32[64]{0:T(128)}, f32[64]{0:T(128)S(1)}, u32[]{:S(2)}) copy-start(f32[64]{0:T(128)S(1)} %get-tuple-element.174) | copy-start | bytes 772
  25.0 64.6 %copy-start.54 = (f32[64]{0:T(128)}, f32[64]{0:T(128)S(1)}, u32[]{:S(2)}) copy-start(f32[64]{0:T(128)S(1)} %get-tuple-element.175) | copy-start | bytes 772
  25.0 64.6 %copy-start.55 = (f32[64]{0:T(128)}, f32[64]{0:T(128)S(1)}, u32[]{:S(2)}) copy-start(f32[64]{0:T(128)S(1)} %get-tuple-element.176) | copy-start | bytes 772
  25.6 64.0 %copy-start.56 = (f32[64]{0:T(128)}, f32[64]{0:T(128)S(1)}, u32[]{:S(2)}) copy-start(f32[64]{0:T(128)S(1)} %get-tuple-element.177) | copy-start | bytes 772
  25.7 64.0 %copy-start.57 = (f32[64]{0:T(128)}, f32[64]{0:T(128)S(1)}, u32[]{:S(2)}) copy-start(f32[64]{0:T(128)S(1)} %get-tuple-element.178) | copy-start | bytes 772
  25.7 64.0 %copy-start.58 = (f32[64]{0:T(128)}, f32[64]{0:T(128)S(1)}, u32[]{:S(2)}) copy-start(f32[64]{0:T(128)S(1)} %get-tuple-element.179) | copy-start | bytes 772
  25.7 64.0 %copy-start.59 = (f32[64]{0:T(128)}, f32[64]{0:T(128)S(1)}, u32[]{:S(2)}) copy-start(f32[64]{0:T(128)S(1)} %get-tuple-element.180) | copy-start | bytes 772
  25.7 64.0 %copy-start.60 = (f32[64]{0:T(128)}, f32[64]{0:T(128)S(1)}, u32[]{:S(2)}) copy-start(f32[64]{0:T(128)S(1)} %get-tuple-element.181) | copy-start | bytes 772
  25.7 64.0 %copy-start.61 = (f32[64]{0:T(128)}, f32[64]{0:T(128)S(1)}, u32[]{:S(2)}) copy-start(f32[64]{0:T(128)S(1)} %get-tuple-element.182) | copy-start | bytes 772
  25.7 64.0 %copy-start.62 = (f32[64]{0:T(128)}, f32[64]{0:T(128)S(1)}, u32[]{:S(2)}) copy-start(f32[64]{0:T(128)S(1)} %get-tuple-element.183) | copy-start | bytes 772
  25.7 64.0 %copy-start.63 = (f32[64]{0:T(128)}, f32[64]{0:T(128)S(1)}, u32[]{:S(2)}) copy-start(f32[64]{0:T(128)S(1)} %get-tuple-element.184) | copy-start | bytes 772
  25.7 64.0 %copy-start.64 = (f32[64]{0:T(128)}, f32[64]{0:T(128)S(1)}, u32[]{:S(2)}) copy-start(f32[64]{0:T(128)S(1)} %get-tuple-element.185) | copy-start | bytes 772
  26.6 61.8 %collective-permute-start.3 = (bf16[1,64,3,134]{1,2,3,0:T(4,128)(2,1)S(1)}, bf16[1,64,3,134]{1,2,3,0:T(4,128)(2,1)S(1)}, u32[]{:S(2)}, u32[]{:S(2)}) collective-permute-start(bf16[1,64,3,134]{1,2,3,0:T(4,128)(2,1)S(1)} %get-tuple-element.151), channel_id=1, source_target_pairs={{1,0},{2,1},{3,2},{4,3},{5,4},{6,5},{7,6},{8,7},{9,8},{10,9},{11,1... | collective-permute-start | bytes 154376 | tf_op jit(solution)/shard_map/ppermute | solution.py:18
  32.5 56.3 %collective-permute-start.2 = (bf16[1,64,3,134]{1,2,3,0:T(4,128)(2,1)S(1)}, bf16[1,64,3,134]{1,2,3,0:T(4,128)(2,1)S(1)}, u32[]{:S(2)}, u32[]{:S(2)}) collective-permute-start(bf16[1,64,3,134]{1,2,3,0:T(4,128)(2,1)S(1)} %get-tuple-element.150), channel_id=1, source_target_pairs={{0,1},{1,2},{2,3},{3,4},{4,5},{5,6},{6,7},{7,8},{8,9},{9,10},{10,1... | collective-permute-start | bytes 154376 | tf_op jit(solution)/shard_map/ppermute | solution.py:16
  121.0 18.5 %copy-start.5 = (f32[1,64,16,128]{3,2,1,0:T(8,128)S(1)}, f32[1,64,16,128]{3,2,1,0:T(8,128)}, u32[]{:S(2)}) copy-start(f32[1,64,16,128]{3,2,1,0:T(8,128)} %copy.108) | copy-start | bytes 1572868
  121.0 18.5 %copy-start.6 = (bf16[256,2048]{0,1:T(8,128)(2,1)S(1)}, bf16[256,2048]{0,1:T(8,128)(2,1)}, u32[]{:S(2)}) copy-start(bf16[256,2048]{0,1:T(8,128)(2,1)} %get-tuple-element.212) | copy-start | bytes 3145732
  121.0 18.5 %copy-start.19 = (f32[2048]{0:T(1024)S(1)}, f32[2048]{0:T(1024)}, u32[]{:S(2)}) copy-start(f32[2048]{0:T(1024)} %get-tuple-element.208) | copy-start | bytes 24580
  121.0 18.6 %copy-start.66 = (f32[64]{0:T(128)S(1)}, f32[64]{0:T(128)}, u32[]{:S(2)}) copy-start(f32[64]{0:T(128)} %convert_element_type.420) | copy-start | bytes 772
  121.2 7.0 %collective-permute-start.4 = (bf16[1,64,16,3]{3,1,2,0:T(8,128)(2,1)S(1)}, bf16[1,64,16,3]{3,1,2,0:T(8,128)(2,1)S(1)}, u32[]{:S(2)}, u32[]{:S(2)}) collective-permute-start(bf16[1,64,16,3]{3,1,2,0:T(8,128)(2,1)S(1)} %get-tuple-element.156), channel_id=1, source_target_pairs={{0,16},{16,32},{32,48},{48,64},{64,80},{80,96},{96,112},{112,128},... | collective-permute-start | bytes 18440 | tf_op jit(solution)/shard_map/ppermute | solution.py:16
  124.5 10.9 %collective-permute-start.5 = (bf16[1,64,16,3]{3,1,2,0:T(8,128)(2,1)S(1)}, bf16[1,64,16,3]{3,1,2,0:T(8,128)(2,1)S(1)}, u32[]{:S(2)}, u32[]{:S(2)}) collective-permute-start(bf16[1,64,16,3]{3,1,2,0:T(8,128)(2,1)S(1)} %get-tuple-element.157), channel_id=1, source_target_pairs={{16,0},{32,16},{48,32},{64,48},{80,64},{96,80},{112,96},{128,112},... | collective-permute-start | bytes 18440 | tf_op jit(solution)/shard_map/ppermute | solution.py:18
  136.2 4.5 collective-permute-start.6
  138.2 6.6 %collective-permute-start.7 = (bf16[1,64,3,134]{3,1,2,0:T(8,128)(2,1)}, bf16[1,64,3,134]{3,1,2,0:T(8,128)(2,1)}, u32[]{:S(2)}, u32[]{:S(2)}) collective-permute-start(bf16[1,64,3,134]{3,1,2,0:T(8,128)(2,1)} %get-tuple-element.146), channel_id=1, source_target_pairs={{1,0},{2,1},{3,2},{4,3},{5,4},{6,5},{7,6},{8,7},{9,8},{10,9},{11,1... | collective-permute-start | bytes 154376 | tf_op jit(solution)/shard_map/ppermute | solution.py:18
  140.6 332.4 %all-gather.5.cloned.1.call-start = ((), (), s32[]{:S(2)}) async-start(), calls=%async_computation.1 | async-start | bytes 1622016 | tf_op jit(solution)/shard_map/all_gather | solution.py:173
  156.3 446.0 %all-reduce.10.cloned.1.call-start = ((), (), s32[]{:S(2)}) async-start(), calls=%async_computation.3 | async-start | bytes 262144 | tf_op jit(solution)/shard_map/psum | solution.py:179
  479.4 10.7 %slice-start = ((f32[1,64,19,128]{3,1,2,0:T(8,128)}), f32[1,64,16,128]{3,1,2,0:T(8,128)S(1)}, s32[]{:S(2)}) async-start(f32[1,64,19,128]{3,1,2,0:T(8,128)} %copy-done.9), calls=%async_computation.4 | async-start | bytes 1048576 | tf_op jit(solution)/shard_map/slice | solution.py:167
  479.4 10.8 %copy-start.17 = (bf16[1,64,16,128]{3,2,1,0:T(8,128)(2,1)S(1)}, bf16[1,64,16,128]{3,2,1,0:T(8,128)(2,1)}, u32[]{:S(2)}) copy-start(bf16[1,64,16,128]{3,2,1,0:T(8,128)(2,1)} %param.14) | copy-start | bytes 786436
  479.4 10.8 %copy-start.22 = (f32[16,128]{1,0:T(8,128)S(1)}, f32[16,128]{1,0:T(8,128)}, u32[]{:S(2)}) copy-start(f32[16,128]{1,0:T(8,128)} %get-tuple-element.207) | copy-start | bytes 24580
  (42 other events, 182.1 us)
Sparse Core Ops, SparseCore 0:
  11.7 67.3 all-gather.2
  140.7 270.7 all-reduce.7
  415.6 57.3 all-gather.4
  476.1 126.1 all-reduce.9
